TPU v7x, 32 devices: a whole 2x2x4 slice. The times are simulated.
32 devices in a mesh: frame: 4 (over y, core), tok: 8 (over z, x).
Axes of the slice: x: 2, y: 2, z: 4, core: 2. Of those that a mesh axis runs over, the one named last changes fastest.
Arguments:
- inputs: bfloat16 [4, 6144, 512], P('frame', 'tok'), may hold values from -16 to 16
- kv_weight: bfloat16 [512, 2048], replicated, may hold values from -0.25 to 0.25
- latent_queries: bfloat16 [1024, 1024], P('tok'), may hold values from -21 to 21
- mix_gain: float32 [3072], replicated, may hold values from 0.5 to 2
- mix_weight: bfloat16 [3072, 1024], P(None, 'tok'), may hold values from -0.109375 to 0.109375
- output_queries: bfloat16 [4, 1024, 1024], P('frame', 'tok'), may hold values from -28 to 28
Outputs:
- decoded: float32 [4, 1024, 1024], P('frame', 'tok')
All inputs are finite; a program needn't handle non-finite values.
Results may differ from a plain program's by a relative error of at most 0.035.
Values may be sent and summed in bfloat16 or wider, within the bound.
A program may use at most 128 MiB of HBM per device.

v0:
```python
import math

import jax
import jax.numpy as jnp
from jax import lax
from jax.sharding import PartitionSpec as P

HEADS = 8
HEAD_DIM = 128


def from_behind(block, axis, distance):
    devices = range(lax.axis_size(axis))
    route = [(i - distance, i) for i in devices if i - distance in devices]
    return lax.ppermute(block, axis, route)


def attend_heads(queries, keys, values, head_count, head_dim):
    maxima = []
    numers = []
    denoms = []
    for head_index in range(head_count):
        low_col = head_index * head_dim
        high_col = low_col + head_dim
        scores = lax.dot_general(
            queries[:, low_col:high_col],
            keys[:, low_col:high_col],
            (((1,), (1,)), ((), ())),
            preferred_element_type=jnp.float32,
        ) / math.sqrt(head_dim)
        row_peak = jnp.max(scores, axis=1)
        weights = jnp.exp(scores - row_peak[:, None])
        denoms.append(jnp.sum(weights, axis=1))
        numers.append(
            jnp.dot(
                weights.astype(jnp.bfloat16),
                values[:, low_col:high_col],
                preferred_element_type=jnp.float32,
            )
        )
        maxima.append(row_peak)
    return (jnp.stack(maxima, axis=1), jnp.concatenate(numers, axis=1), jnp.stack(denoms, axis=1))


def finish_latents(numerator, denominator, head_count, head_dim):
    row_count = numerator.shape[0]
    shaped = numerator.reshape(row_count, head_count, head_dim) / denominator[:, :, None]
    return shaped.reshape(row_count, head_count * head_dim).astype(jnp.bfloat16)


def project_cols(latent_part, gain_part, weight_part):
    scaled = (latent_part.astype(jnp.float32) * gain_part).astype(jnp.bfloat16)
    return lax.dot_general(
        weight_part, scaled, (((0,), (1,)), ((), ())), preferred_element_type=jnp.float32
    )


def local(inputs, kv_weight, latent_queries, mix_gain, mix_weight, output_queries):
    head_count = HEADS
    head_dim = HEAD_DIM
    latent_width = head_count * head_dim
    frame_inputs = inputs[0]
    queries = lax.all_gather(latent_queries, "tok", axis=0, tiled=True)
    key_values = jnp.dot(frame_inputs, kv_weight, preferred_element_type=jnp.float32).astype(
        jnp.bfloat16
    )
    maxima, numers, denoms = attend_heads(
        queries, key_values[:, :latent_width], key_values[:, latent_width:], head_count, head_dim
    )
    peak_all = lax.pmax(maxima.astype(jnp.bfloat16), "tok").astype(maxima.dtype)
    rescale = jnp.exp(maxima - peak_all)
    latent_count = queries.shape[0]
    numer_terms = (
        numers.reshape(latent_count, head_count, head_dim) * rescale[:, :, None]
    ).reshape(latent_count, latent_width)
    denom_terms = denoms * rescale
    numerator, denominator = (
        lax.psum(numer_terms.astype(jnp.bfloat16), "tok").astype(jnp.float32),
        lax.psum(denom_terms.astype(jnp.bfloat16), "tok").astype(jnp.float32),
    )
    latents = finish_latents(numerator, denominator, head_count, head_dim)
    latent_f32 = latents.astype(jnp.float32)
    own_squares = jnp.sum(latent_f32 * latent_f32, axis=1)
    term_now = project_cols(latents, mix_gain[:latent_width], mix_weight[:latent_width])
    term_one, squares_one = (
        from_behind(
            project_cols(
                latents,
                mix_gain[latent_width : 2 * latent_width],
                mix_weight[latent_width : 2 * latent_width],
            ).astype(jnp.bfloat16),
            "frame",
            1,
        ).astype(jnp.float32),
        from_behind(own_squares.astype(jnp.bfloat16), "frame", 1).astype(own_squares.dtype),
    )
    term_two, squares_two = (
        from_behind(
            project_cols(
                latents, mix_gain[2 * latent_width :], mix_weight[2 * latent_width :]
            ).astype(jnp.bfloat16),
            "frame",
            2,
        ).astype(jnp.float32),
        from_behind(own_squares.astype(jnp.bfloat16), "frame", 2).astype(own_squares.dtype),
    )
    summed = term_now + term_one + term_two
    squares = own_squares + squares_one + squares_two
    inverse = lax.rsqrt(squares / (3 * latent_width) + 1e-06)
    mixed_cols = jax.nn.gelu(summed * inverse[None, :], approximate=False).astype(jnp.bfloat16)
    mixed_t = lax.all_gather(mixed_cols, "tok", axis=0, tiled=True)
    frame_queries = output_queries[0]
    pieces = []
    for head_index in range(head_count):
        low_col = head_index * head_dim
        high_col = low_col + head_dim
        scores = jnp.dot(
            frame_queries[:, low_col:high_col],
            mixed_t[low_col:high_col],
            preferred_element_type=jnp.float32,
        ) / math.sqrt(head_dim)
        row_peak = jnp.max(scores, axis=1)
        weights = jnp.exp(scores - row_peak[:, None])
        denom_sum = jnp.sum(weights, axis=1)
        head_sum = lax.dot_general(
            weights.astype(jnp.bfloat16),
            mixed_t[low_col:high_col],
            (((1,), (1,)), ((), ())),
            preferred_element_type=jnp.float32,
        )
        pieces.append(head_sum / denom_sum[:, None])
    result = jnp.concatenate(pieces, axis=1)
    return result[None]


def solution(mesh):
    return jax.shard_map(
        local,
        mesh=mesh,
        in_specs=(
            P("frame", "tok", None),
            P(),
            P("tok", None),
            P(),
            P(None, "tok"),
            P("frame", "tok", None),
        ),
        out_specs=P("frame", "tok", None),
        check_vma=False,
    )
```

profile of v0, /device:TPU:4, one launch (start us, length us, event | category | flops | bytes accessed | tf_op | source)
XLA Modules:
  0.0 333.6 jit_solution(3611206243185878491)
XLA Ops:
  8.1 4.6 %convolution_convert_fusion = bf16[768,2048]{1,0:T(8,128)(2,1)} fusion(bf16[512,2048]{1,0:T(8,128)(2,1)S(1)} %copy-done, bf16[1,768,512]{2,1,0:T(8,128)(2,1)} %param.6), kind=kOutput, calls=%fused_computation.12 | convolution fusion | flops 1612185600 | bytes 6029312 | tf_op jit(solution)/shard_map/dot_general | solution.py:64
  12.7 47.3 %all-gather.3.cloned.1.call-done = bf16[1024,1024]{1,0:T(8,128)(2,1)} async-done(((bf16[128,1024]{1,0:T(8,128)(2,1)}), bf16[1024,1024]{1,0:T(8,128)(2,1)}) %all-gather.3.cloned.1.call-update) | async-done | bytes 2097168 | tf_op jit(solution)/shard_map/all_gather | solution.py:63
  62.2 2.4 fusion.63
  66.8 2.1 multiply_reduce_fusion.5
  69.5 2.1 multiply_reduce_fusion.4
  74.9 2.1 multiply_reduce_fusion.2
  77.5 2.1 multiply_reduce_fusion.1
  80.2 2.1 multiply_reduce_fusion
  84.7 34.7 %pmax.7 = bf16[1024,8]{0,1:T(8,128)(2,1)S(1)} all-reduce(bf16[1024,8]{0,1:T(8,128)(2,1)S(1)} %convert_element_type.143), channel_id=1, replica_groups=mesh['frame'=4,'tok'=8] {'tok'}, use_global_device_ids=true, to_apply=%region_8.0 | all-reduce | flops 8192 | bytes 32768 | tf_op jit(solution)/shard_map/pmax | solution.py:70
  119.3 3.6 %fusion.66 = f32[1024,1024]{0,1:T(8,128)} fusion(f32[1024,1024]{0,1:T(8,128)} %fusion.63, f32[768,1024]{1,0:T(8,128)} %copy-done.1, f32[1024]{0:T(1024)S(1)} %get-tuple-element.14, bf16[768,2048]{1,0:T(8,128)(2,1)} %convolution_convert_fusion), kind=kOutput, calls=%fused_computation.76 | convolution fusion | flops 203685888 | bytes 3870720 | tf_op jit(solution)/shard_map/dot_general | solution.py:35
  122.9 2.6 fusion.69
  125.5 2.6 fusion.72
  128.1 2.6 fusion.75
  130.7 2.6 fusion.78
  133.3 2.4 fusion.81
  135.7 2.4 fusion.84
  138.2 4.1 %fusion.5 = bf16[1024,1024]{0,1:T(8,128)(2,1)} fusion(f32[1024,1024]{0,1:T(8,128)} %fusion.84, f32[1024,8]{0,1:T(8,128)S(1)} %get-tuple-element.8), kind=kLoop, calls=%fused_computation.11 | loop fusion | flops 2097152 | bytes 6324224 | tf_op jit(solution)/shard_map/convert_element_type | solution.py:78
  142.5 34.5 %psum.15 = bf16[1024,8]{0,1:T(8,128)(2,1)S(1)} all-reduce(bf16[1024,8]{0,1:T(8,128)(2,1)S(1)} %get-tuple-element.7), channel_id=1, replica_groups=mesh['frame'=4,'tok'=8] {'tok'}, use_global_device_ids=true, to_apply=%region_18.0 | all-reduce | flops 8192 | bytes 32768 | tf_op jit(solution)/shard_map/psum | solution.py:79
  177.0 64.9 %all-reduce.2.cloned.1.call-done = bf16[1024,1024]{0,1:T(8,128)(2,1)} async-done(((bf16[1024,1024]{0,1:T(8,128)(2,1)}), bf16[1024,1024]{0,1:T(8,128)(2,1)}) %all-reduce.2.cloned.1.call-update) | async-done | bytes 2097168 | tf_op jit(solution)/shard_map/psum | solution.py:78
  241.9 2.3 fusion.3
  250.9 2.1 collective-permute-start.2
  253.0 3.4 %collective-permute-done.3 = bf16[1024]{0:T(1024)(128)(2,1)S(1)} collective-permute-done((bf16[1024]{0:T(1024)(128)(2,1)S(1)}, bf16[1024]{0:T(1024)(128)(2,1)S(1)}, u32[]{:S(2)}, u32[]{:S(2)}) %collective-permute-start.3) | collective-permute-done | bytes 2080 | tf_op jit(solution)/shard_map/ppermute | solution.py:15
  257.9 2.9 fusion.113
  260.8 51.2 %all-gather.5.cloned.1.call-done = bf16[1024,1024]{0,1:T(8,128)(2,1)} async-done(((bf16[128,1024]{0,1:T(8,128)(2,1)}), bf16[1024,1024]{0,1:T(8,128)(2,1)}) %all-gather.5.cloned.1.call-update) | async-done | bytes 2097168 | tf_op jit(solution)/shard_map/all_gather | solution.py:111
  (92 shorter events, 36.4 us)
Async XLA Ops:
  6.5 1.6 copy-start
  6.5 53.5 %all-gather.3.cloned.1.call-start = ((), (), s32[]{:S(2)}) async-start(), calls=%async_computation | async-start | bytes 2359296 | tf_op jit(solution)/shard_map/all_gather | solution.py:63
  7.3 234.6 %all-reduce.2.cloned.1.call-start = ((), (), s32[]{:S(2)}) async-start(), calls=%async_computation.1 | async-start | bytes 4194304 | tf_op jit(solution)/shard_map/psum | solution.py:78
  66.3 2.7 copy-start.1
  68.9 2.7 copy-start.2
  71.6 2.7 copy-start.4
  74.3 2.7 copy-start.6
  77.0 2.7 copy-start.8
  79.6 2.7 copy-start.10
  82.3 1.7 copy-start.12
  119.3 3.6 %copy-start.3 = (f32[768,1024]{1,0:T(8,128)S(1)}, f32[768,1024]{1,0:T(8,128)}, u32[]{:S(2)}) copy-start(f32[768,1024]{1,0:T(8,128)} %copy-done.2) | copy-start | bytes 9437188
  119.3 6.2 %copy-start.5 = (f32[768,1024]{1,0:T(8,128)S(1)}, f32[768,1024]{1,0:T(8,128)}, u32[]{:S(2)}) copy-start(f32[768,1024]{1,0:T(8,128)} %copy-done.4) | copy-start | bytes 9437188
  122.9 5.2 %copy-start.7 = (f32[768,1024]{1,0:T(8,128)S(1)}, f32[768,1024]{1,0:T(8,128)}, u32[]{:S(2)}) copy-start(f32[768,1024]{1,0:T(8,128)} %copy-done.6) | copy-start | bytes 9437188
  125.5 5.2 %copy-start.9 = (f32[768,1024]{1,0:T(8,128)S(1)}, f32[768,1024]{1,0:T(8,128)}, u32[]{:S(2)}) copy-start(f32[768,1024]{1,0:T(8,128)} %copy-done.8) | copy-start | bytes 9437188
  128.1 5.2 %copy-start.11 = (f32[768,1024]{1,0:T(8,128)S(1)}, f32[768,1024]{1,0:T(8,128)}, u32[]{:S(2)}) copy-start(f32[768,1024]{1,0:T(8,128)} %copy-done.10) | copy-start | bytes 9437188
  130.7 5.0 %copy-start.13 = (f32[768,1024]{1,0:T(8,128)S(1)}, f32[768,1024]{1,0:T(8,128)}, u32[]{:S(2)}) copy-start(f32[768,1024]{1,0:T(8,128)} %copy-done.12) | copy-start | bytes 9437188
  138.2 4.2 %copy-start.15 = (f32[3072]{0:T(1024)S(1)}, f32[3072]{0:T(1024)}, u32[]{:S(2)}) copy-start(f32[3072]{0:T(1024)} %param.9) | copy-start | bytes 36868
  142.4 101.9 %copy-start.16 = (bf16[3072,128]{1,0:T(8,128)(2,1)S(1)}, bf16[3072,128]{1,0:T(8,128)(2,1)}, u32[]{:S(2)}) copy-start(bf16[3072,128]{1,0:T(8,128)(2,1)} %param.10) | copy-start | bytes 2359300
  142.4 169.6 %all-gather.5.cloned.1.call-start = ((), (), s32[]{:S(2)}) async-start(), calls=%async_computation.2 | async-start | bytes 2359296 | tf_op jit(solution)/shard_map/all_gather | solution.py:111
  245.3 12.6 %collective-permute-start.1 = (bf16[128,1024]{0,1:T(8,128)(2,1)S(1)}, bf16[128,1024]{0,1:T(8,128)(2,1)S(1)}, u32[]{:S(2)}, u32[]{:S(2)}) collective-permute-start(bf16[128,1024]{0,1:T(8,128)(2,1)S(1)} %fusion.96), channel_id=1, source_target_pairs={{0,16},{8,24},{1,17},{9,25},{2,18},{10,26},{3,19},{11,27},{4,20},{... | collective-permute-start | bytes 786440 | tf_op jit(solution)/shard_map/ppermute | solution.py:15
  247.6 10.2 %collective-permute-start = (bf16[128,1024]{0,1:T(8,128)(2,1)S(1)}, bf16[128,1024]{0,1:T(8,128)(2,1)S(1)}, u32[]{:S(2)}, u32[]{:S(2)}) collective-permute-start(bf16[128,1024]{0,1:T(8,128)(2,1)S(1)} %fusion.99), channel_id=1, source_target_pairs={{0,8},{8,16},{16,24},{1,9},{9,17},{17,25},{2,10},{10,18},{18,26},{... | collective-permute-start | bytes 786440 | tf_op jit(solution)/shard_map/ppermute | solution.py:15
  249.6 6.9 %collective-permute-start.3 = (bf16[1024]{0:T(1024)(128)(2,1)S(1)}, bf16[1024]{0:T(1024)(128)(2,1)S(1)}, u32[]{:S(2)}, u32[]{:S(2)}) collective-permute-start(bf16[1024]{0:T(1024)(128)(2,1)S(1)} %convert_element_type.160), channel_id=1, source_target_pairs={{0,16},{8,24},{1,17},{9,25},{2,18},{10,26},{3,19},{11,27},{4,20},{... | collective-permute-start | bytes 6152 | tf_op jit(solution)/shard_map/ppermute | solution.py:15
  250.9 7.0 %collective-permute-start.2 = (bf16[1024]{0:T(1024)(128)(2,1)S(1)}, bf16[1024]{0:T(1024)(128)(2,1)S(1)}, u32[]{:S(2)}, u32[]{:S(2)}) collective-permute-start(bf16[1024]{0:T(1024)(128)(2,1)S(1)} %convert_element_type.160), channel_id=1, source_target_pairs={{0,8},{8,16},{16,24},{1,9},{9,17},{17,25},{2,10},{10,18},{18,26},{... | collective-permute-start | bytes 6152 | tf_op jit(solution)/shard_map/ppermute | solution.py:15
  317.6 6.0 %copy-start.14 = (bf16[1024,1024]{0,1:T(8,128)(2,1)S(1)}, bf16[1024,1024]{0,1:T(8,128)(2,1)}, u32[]{:S(2)}) copy-start(bf16[1024,1024]{0,1:T(8,128)(2,1)} %all-gather.5.cloned.1.call-done) | copy-start | bytes 6291460
Sparse Core Ops, SparseCore 0:
  9.5 50.4 all-gather.2
  142.5 99.3 all-reduce.1
  260.9 51.0 all-gather.4
where the time goes:
time: 336 us; the launch traced here: 334 us
  waiting for transfers between devices  169 us (50%)
  blocking collectives  69.2 us (21%)
  matrix products  59.3 us (18%)
  between operations  13.4 us (4%)
  other arithmetic  12.2 us (4%)
  starting transfers between devices  6.73 us (2%)
  local copies, waits for them, and re-layouts  3.73 us (1%)
    psum x1, waiting for transfers between devices, local(): lax.psum(numer_terms.astype(jnp.bfloat16), 'tok').astype(jnp.float32)  64.9 us
    all_gather x1, waiting for transfers between devices, local(): mixed_t = lax.all_gather(mixed_cols, 'tok', axis=0, tiled=True)  51.2 us
    all_gather x1, waiting for transfers between devices, local(): queries = lax.all_gather(latent_queries, 'tok', axis=0, tiled=True)  47.3 us
    pmax x1, blocking collectives, local(): peak_all = lax.pmax(maxima.astype(jnp.bfloat16), 'tok').astype(maxima.dtype)  34.7 us
    psum x1, blocking collectives, local(): lax.psum(denom_terms.astype(jnp.bfloat16), 'tok').astype(jnp.float32)  34.5 us
    dot_general x8, matrix products, attend_heads(): jnp.dot(weights.astype(jnp.bfloat16), values[:, low_col:high_col], prefer...  21.2 us
    dot_general x8, matrix products, attend_heads(): lax.dot_general(queries[:, low_col:high_col], keys[:, low_col:high_col],...  15.8 us
    dot_general x8, matrix products, local(): jnp.dot(frame_queries[:, low_col:high_col], mixed_t[low_col:high_col], pr...  10.2 us
  transfers between devices with their start and end apart: 7, of which 5 were waited for; matrix products, arithmetic and copies ran while one was open for 2% of the time, Pallas kernels for 0%

commit v1 on v0

--- a/solution.py
+++ b/solution.py
@@ -1,8 +1,11 @@
+import functools
 import math
 
 import jax
 import jax.numpy as jnp
 from jax import lax
+from jax.experimental import pallas as pl
+from jax.experimental.pallas import tpu as pltpu
 from jax.sharding import PartitionSpec as P
 
 HEADS = 8
@@ -133,9 +136,368 @@
     return result[None]
 
 
+MESH = pl.DeviceIdType.MESH
+LOG2E = 1.4426950408889634
+
+
+def dot_nt(a, b):
+    return lax.dot_general(a, b, (((1,), (1,)), ((), ())), preferred_element_type=jnp.float32)
+
+
+def attend_columns(keys, values_t, queries, factor):
+    scores = dot_nt(keys, queries)
+    if factor is not None:
+        scores = scores * factor
+    peak = jnp.max(scores, axis=0, keepdims=True)
+    weights = jnp.exp2(scores - peak)
+    denom = jnp.sum(weights, axis=0, keepdims=True)
+    numer = jnp.dot(values_t, weights.astype(jnp.bfloat16), preferred_element_type=jnp.float32)
+    return numer, peak, denom
+
+
+def copy_ids(n_tok, pairs):
+    names = []
+    for j in range(1, pairs):
+        names += [("qz", j), ("qx", j), ("nz", j), ("sz", j), ("lz", j), ("lx", j)]
+    for j in range(pairs):
+        names += [("nx", j), ("sx", j), ("t1", j), ("t2", j)]
+    for k in range(1, n_tok):
+        names += [("qc", k), ("oq", k), ("out", k)]
+    names += [("qx", 0), ("lx", 0)]
+    return {name: i for i, name in enumerate(names)}
+
+
+def window_kernel(
+    n_tok, n_frame, x_ref, kvw_ref, lq_ref, gain_ref, w_ref, oq_ref, out_ref,
+    qbuf, kbuf, vbuf, w3, own_n, own_s, xs_n, xs_s, xr_n, xr_s, zs_n, zs_s, zr_n, zr_s,
+    lat, now, sq_own, ts1, ts2, tr1, tr2, mix_t, mix, oqbuf, osend, obuf, send_sem, recv_sem,
+):
+    heads = n_tok
+    pairs = n_tok // 2
+    rows = lq_ref.shape[0]
+    dim = w_ref.shape[1]
+    width = heads * dim
+    qrows = oq_ref.shape[1]
+    factor = LOG2E / math.sqrt(dim)
+    ids = copy_ids(n_tok, pairs)
+    fi = lax.axis_index("frame")
+    ti = lax.axis_index("tok")
+    half = rows // 2
+    mine = lax.rem(fi, 2)
+    sibling = fi + 1 - 2 * mine
+    started = []
+
+    def flip(k):
+        out = 0
+        bit = 1
+        while bit < n_tok:
+            b = lax.rem(lax.div(ti, bit), 2)
+            out = out + bit * ((1 - b) if (k & bit) else b)
+            bit *= 2
+        return out
+
+    peer = [flip(k) for k in range(n_tok)]
+
+    def copy(name, src, dst, where):
+        i = ids[name]
+        return pltpu.make_async_remote_copy(
+            src_ref=src, dst_ref=dst, send_sem=send_sem.at[i], recv_sem=recv_sem.at[i],
+            device_id=where, device_id_type=MESH,
+        )
+
+    def send(name, src, dst, where):
+        c = copy(name, src, dst, where)
+        c.start()
+        started.append(c)
+
+    def arrived(name, dst, where):
+        copy(name, dst, dst, where).wait_recv()
+
+    def tok(k):
+        return (fi, peer[k])
+
+    barrier = pltpu.get_barrier_semaphore()
+    for k in range(1, n_tok):
+        pl.semaphore_signal(barrier, inc=1, device_id=tok(k), device_id_type=MESH)
+    for o in range(1, n_frame):
+        pl.semaphore_signal(
+            barrier, inc=1, device_id=(lax.rem(fi + o, n_frame), ti), device_id_type=MESH
+        )
+    pl.semaphore_wait(barrier, n_tok - 1 + n_frame - 1)
+
+    here = pl.multiple_of(mine * half, half)
+    there = pl.multiple_of((1 - mine) * half, half)
+
+    def qpart(k, off):
+        return qbuf.at[pl.ds(k * rows + off, half), :]
+
+    own_half = lq_ref.at[pl.ds(here, half), :]
+    for j in range(pairs - 1, 0, -1):
+        send(("qz", j), own_half, qpart(2 * j, here), tok(2 * j))
+    send(("qx", 0), own_half, qpart(1, here), tok(1))
+    for k in range(n_tok - 1, 0, -1):
+        cols = pl.ds(pl.multiple_of(peer[k] * dim, dim), dim)
+        send(("oq", k), oq_ref.at[0, :, cols], oqbuf.at[pl.ds(k * qrows, qrows), :], tok(k))
+    qbuf[0:rows, :] = lq_ref[...]
+    own_cols = pl.ds(pl.multiple_of(ti * dim, dim), dim)
+    oqbuf[0:qrows, :] = oq_ref[0, :, own_cols]
+
+    def project_keys(i, carry):
+        cols = pl.ds(pl.multiple_of(i * 2 * dim, 2 * dim), 2 * dim)
+        k = jnp.dot(x_ref[0], kvw_ref[:, cols], preferred_element_type=jnp.float32)
+        k = (k * factor).astype(jnp.bfloat16)
+        kbuf[2 * i] = k[:, :dim]
+        kbuf[2 * i + 1] = k[:, dim:]
+        return carry
+
+    lax.fori_loop(0, heads // 2, project_keys, 0)
+
+    arrived(("qx", 0), qpart(1, here), tok(1))
+    send(("qc", 1), qpart(1, here), qpart(1, here), (sibling, ti))
+    for j in range(pairs - 1, 0, -1):
+        arrived(("qz", j), qpart(2 * j, here), tok(2 * j))
+        send(("qx", j), qpart(2 * j, here), qpart(2 * j + 1, here), tok(1))
+        send(("qc", 2 * j), qpart(2 * j, here), qpart(2 * j, here), (sibling, ti))
+
+    def project_values(i, carry):
+        cols = pl.ds(pl.multiple_of(width + i * 2 * dim, 2 * dim), 2 * dim)
+        v = jnp.dot(x_ref[0], kvw_ref[:, cols], preferred_element_type=jnp.float32)
+        v = v.astype(jnp.bfloat16).T
+        vbuf[2 * i] = v[:dim]
+        vbuf[2 * i + 1] = v[dim:]
+        return carry
+
+    lax.fori_loop(0, heads // 2, project_values, 0)
+
+    for j in range(pairs - 1, 0, -1):
+        k = 2 * j + 1
+        arrived(("qx", j), qpart(k, here), tok(1))
+        send(("qc", k), qpart(k, here), qpart(k, here), (sibling, ti))
+
+    for t in range(3):
+        w_t = w_ref[t * width : (t + 1) * width, :].T.astype(jnp.float32)
+        w3[t * dim : (t + 1) * dim, :] = (w_t * gain_ref[t : t + 1, :]).astype(jnp.bfloat16)
+
+    def merge_x(j):
+        arrived(("nx", j), xr_n.at[j], tok(1))
+        arrived(("sx", j), xr_s.at[j], tok(1))
+        m1, l1 = own_s[j, 0:heads, :], own_s[j, heads : 2 * heads, :]
+        m2, l2 = xr_s[j, 0:heads, :], xr_s[j, heads : 2 * heads, :]
+        m = jnp.maximum(m1, m2)
+        a1, a2 = jnp.exp2(m1 - m), jnp.exp2(m2 - m)
+        l = l1 * a1 + l2 * a2
+        if j == 0:
+            own_s[0, 0:heads, :] = m
+            own_s[0, heads : 2 * heads, :] = l
+        else:
+            zs_s[j, 0:heads, :] = m
+            zs_s[j, heads : 2 * heads, :] = l
+        for h in range(heads):
+            n = own_n[j, h] * a1[h : h + 1] + xr_n[j, h].astype(jnp.float32) * a2[h : h + 1]
+            if j == 0:
+                own_n[0, h] = n
+            else:
+                zs_n[j, h] = n.astype(jnp.bfloat16)
+        if j > 0:
+            send(("nz", j), zs_n.at[j], zr_n.at[j], tok(2 * j))
+            send(("sz", j), zs_s.at[j], zr_s.at[j], tok(2 * j))
+
+    for j in range(pairs - 1, -1, -1):
+        for k in (2 * j, 2 * j + 1):
+            if k > 0:
+                arrived(("qc", k), qpart(k, there), (sibling, ti))
+
+        def head_pair(i, carry, j=j):
+            for u in range(2):
+                h = 2 * i + u
+                cols = pl.ds(pl.multiple_of(h * dim, dim), dim)
+                q = qbuf[2 * j * rows : (2 * j + 2) * rows, cols]
+                n, m, l = attend_columns(kbuf[h], vbuf[h], q, None)
+                own_n[j, h] = n[:, :rows]
+                own_s[j, pl.ds(h, 1), :] = m[:, :rows]
+                own_s[j, pl.ds(heads + h, 1), :] = l[:, :rows]
+                xs_n[j, h] = n[:, rows:].astype(jnp.bfloat16)
+                xs_s[j, pl.ds(h, 1), :] = m[:, rows:]
+                xs_s[j, pl.ds(heads + h, 1), :] = l[:, rows:]
+            return carry
+
+        lax.fori_loop(0, heads // 2, head_pair, 0)
+        send(("nx", j), xs_n.at[j], xr_n.at[j], tok(1))
+        send(("sx", j), xs_s.at[j], xr_s.at[j], tok(1))
+        if j < pairs - 1:
+            merge_x(j + 1)
+    merge_x(0)
+
+    for j in range(pairs - 1, 0, -1):
+        arrived(("nz", j), zr_n.at[j], tok(2 * j))
+        arrived(("sz", j), zr_s.at[j], tok(2 * j))
+    peaks = [own_s[0, 0:heads, :]] + [zr_s[j, 0:heads, :] for j in range(1, pairs)]
+    dens = [own_s[0, heads : 2 * heads, :]]
+    dens += [zr_s[j, heads : 2 * heads, :] for j in range(1, pairs)]
+    top = functools.reduce(jnp.maximum, peaks)
+    scale = [jnp.exp2(p - top) for p in peaks]
+    total = sum(d * s for d, s in zip(dens, scale))
+    scale = [s / total for s in scale]
+    for h in range(heads):
+        n = own_n[0, h] * scale[0][h : h + 1]
+        for j in range(1, pairs):
+            n = n + zr_n[j, h].astype(jnp.float32) * scale[j][h : h + 1]
+        lat[0, h * dim : (h + 1) * dim, :] = n.astype(jnp.bfloat16)
+
+    for j in range(pairs - 1, 0, -1):
+        send(("lz", j), lat.at[0], lat.at[2 * j], tok(2 * j))
+    send(("lx", 0), lat.at[0], lat.at[1], tok(1))
+
+    def mix_pair(c):
+        both = jnp.concatenate([lat[2 * c], lat[2 * c + 1]], axis=1)
+        wide = both.astype(jnp.float32)
+        squares = jnp.sum(wide * wide, axis=0, keepdims=True)
+        terms = jnp.dot(w3[...], both, preferred_element_type=jnp.float32)
+        now[c] = terms[:dim]
+        sq_own[c] = jnp.broadcast_to(squares, sq_own.shape[1:])
+        sq = jnp.broadcast_to(squares, (16, 2 * rows)).astype(jnp.bfloat16)
+        ts1[c, 0:dim, :] = terms[dim : 2 * dim].astype(jnp.bfloat16)
+        ts1[c, dim : dim + 16, :] = sq
+        ts2[c, 0:dim, :] = terms[2 * dim :].astype(jnp.bfloat16)
+        ts2[c, dim : dim + 16, :] = sq
+
+        @pl.when(fi < n_frame - 1)
+        def _():
+            copy(("t1", c), ts1.at[c], tr1.at[c], (lax.rem(fi + 1, n_frame), ti)).start()
+
+        @pl.when(fi < n_frame - 2)
+        def _():
+            copy(("t2", c), ts2.at[c], tr2.at[c], (lax.rem(fi + 2, n_frame), ti)).start()
+
+    order = [1, 2, 3] if pairs == 4 else list(range(1, pairs))
+    for j in order:
+        arrived(("lz", j), lat.at[2 * j], tok(2 * j))
+        send(("lx", j), lat.at[2 * j], lat.at[2 * j + 1], tok(1))
+    for c in [0] + order:
+        arrived(("lx", c), lat.at[2 * c + 1], tok(1))
+        mix_pair(c)
+
+    @pl.when(fi < 1)
+    def _():
+        tr1[...] = jnp.zeros_like(tr1)
+
+    @pl.when(fi < 2)
+    def _():
+        tr2[...] = jnp.zeros_like(tr2)
+
+    for c in [0] + order:
+
+        @pl.when(fi >= 1)
+        def _():
+            copy(("t1", c), ts1.at[c], tr1.at[c], (lax.rem(fi + 1, n_frame), ti)).wait_recv()
+
+        @pl.when(fi >= 2)
+        def _():
+            copy(("t2", c), ts2.at[c], tr2.at[c], (lax.rem(fi + 2, n_frame), ti)).wait_recv()
+
+        summed = now[c] + tr1[c, 0:dim, :].astype(jnp.float32) + tr2[c, 0:dim, :].astype(jnp.float32)
+        squares = (
+            sq_own[c, 0:1, :]
+            + tr1[c, dim : dim + 16, :].astype(jnp.float32)[0:1]
+            + tr2[c, dim : dim + 16, :].astype(jnp.float32)[0:1]
+        )
+        z = summed * lax.rsqrt(squares / (3 * width) + 1e-06)
+        mixed = (0.5 * z * (1.0 + lax.erf(z * math.sqrt(0.5)))).astype(jnp.bfloat16)
+        mix_t[:, c * 2 * rows : (c + 1) * 2 * rows] = mixed
+        mix[c * 2 * rows : (c + 1) * 2 * rows, :] = mixed.T
+
+    for k in range(1, n_tok):
+        arrived(("oq", k), oqbuf.at[pl.ds(k * qrows, qrows), :], tok(k))
+    for c in range(pairs - 1, -1, -1):
+        q = oqbuf[2 * c * qrows : (2 * c + 2) * qrows, :]
+        n, m, l = attend_columns(mix[...], mix_t[...], q, factor)
+        o = (n / l).T
+        for k in (2 * c, 2 * c + 1):
+            part = o[(k - 2 * c) * qrows : (k - 2 * c + 1) * qrows]
+            if k == 0:
+                out_ref[0, :, own_cols] = part
+            else:
+                osend[k] = part.astype(jnp.bfloat16)
+                send(("out", k), osend.at[k], obuf.at[k], tok(k))
+    for k in range(n_tok - 1, 0, -1):
+        arrived(("out", k), obuf.at[k], tok(k))
+        cols = pl.ds(pl.multiple_of(peer[k] * dim, dim), dim)
+        out_ref[0, :, cols] = obuf[k].astype(jnp.float32)
+
+    for c in started:
+        c.wait_send()
+    for c in range(pairs):
+
+        @pl.when(fi < n_frame - 1)
+        def _():
+            copy(("t1", c), ts1.at[c], tr1.at[c], (lax.rem(fi + 1, n_frame), ti)).wait_send()
+
+        @pl.when(fi < n_frame - 2)
+        def _():
+            copy(("t2", c), ts2.at[c], tr2.at[c], (lax.rem(fi + 2, n_frame), ti)).wait_send()
+
+
+def local_fused(inputs, kv_weight, latent_queries, mix_gain, mix_weight, output_queries):
+    n_tok = lax.axis_size("tok")
+    n_frame = lax.axis_size("frame")
+    pairs = n_tok // 2
+    heads = HEADS
+    dim = HEAD_DIM
+    width = heads * dim
+    n_in = inputs.shape[1]
+    rows = latent_queries.shape[0]
+    qrows = output_queries.shape[1]
+    bf16, f32 = jnp.bfloat16, jnp.float32
+    stats = (pairs, 2 * heads, rows)
+    block = (pairs, heads, dim, rows)
+    n_ids = len(copy_ids(n_tok, pairs))
+    vmem = pltpu.VMEM
+    scratch = [
+        vmem((n_tok * rows, width), bf16),
+        vmem((heads, n_in, dim), bf16),
+        vmem((heads, dim, n_in), bf16),
+        vmem((3 * dim, width), bf16),
+        vmem(block, f32), vmem(stats, f32),
+        vmem(block, bf16), vmem(stats, f32),
+        vmem(block, bf16), vmem(stats, f32),
+        vmem(block, bf16), vmem(stats, f32),
+        vmem(block, bf16), vmem(stats, f32),
+        vmem((n_tok, width, rows), bf16),
+        vmem((pairs, dim, 2 * rows), f32),
+        vmem((pairs, 8, 2 * rows), f32),
+        vmem((pairs, dim + 16, 2 * rows), bf16),
+        vmem((pairs, dim + 16, 2 * rows), bf16),
+        vmem((pairs, dim + 16, 2 * rows), bf16),
+        vmem((pairs, dim + 16, 2 * rows), bf16),
+        vmem((dim, n_tok * rows), bf16),
+        vmem((n_tok * rows, dim), bf16),
+        vmem((n_tok * qrows, dim), bf16),
+        vmem((n_tok, qrows, dim), bf16),
+        vmem((n_tok, qrows, dim), bf16),
+        pltpu.SemaphoreType.DMA((n_ids,)),
+        pltpu.SemaphoreType.DMA((n_ids,)),
+    ]
+    return pl.pallas_call(
+        functools.partial(window_kernel, n_tok, n_frame),
+        out_shape=jax.ShapeDtypeStruct((1, qrows, width), f32),
+        in_specs=[pl.BlockSpec(memory_space=pltpu.VMEM)] * 6,
+        out_specs=pl.BlockSpec(memory_space=pltpu.VMEM),
+        scratch_shapes=scratch,
+        compiler_params=pltpu.CompilerParams(
+            collective_id=0, has_side_effects=True, vmem_limit_bytes=56 * 1024 * 1024
+        ),
+    )(inputs, kv_weight, latent_queries, mix_gain.reshape(3, width), mix_weight, output_queries)
+
+
+def pick_local(mesh):
+    n_tok, n_frame = mesh.shape["tok"], mesh.shape["frame"]
+    fits = n_tok == HEADS and n_frame % 2 == 0 and n_frame > 2
+    return local_fused if fits else local
+
+
 def solution(mesh):
     return jax.shard_map(
-        local,
+        pick_local(mesh),
         mesh=mesh,
         in_specs=(
             P("frame", "tok", None),

time: 336 us -> 114 us (0.34)
  waiting for transfers between devices: 169 us -> 0 us
  Pallas kernels: 0 us -> 109 us
  blocking collectives: 69.2 us -> 0 us
  matrix products: 59.3 us -> 0 us
  between operations: 13.4 us -> 0.01 us
  other arithmetic: 12.2 us -> 0 us
  starting transfers between devices: 6.73 us -> 0 us
    pallas_call x0 -> x1, Pallas kernels: none -> 109 us  [local_fused(): pl.pallas_call(functools.partial(window_kernel, n_tok, n_frame), out_shap...]
    all_gather x2 -> x0, waiting for transfers between devices: 98.5 us -> none  [the longest x1 51.2 us: local(): mixed_t = lax.all_gather(mixed_cols, 'tok', axis=0, tiled=True)]
    psum x1 -> x0, waiting for transfers between devices: 64.9 us -> none  [local(): lax.psum(numer_terms.astype(jnp.bfloat16), 'tok').astype(jnp.float32)]
    dot_general x36 -> x0, matrix products: 59.3 us -> none  [the longest x8 21.2 us: attend_heads(): jnp.dot(weights.astype(jnp.bfloat16), values[:, low_col:high_col], prefer...]
    pmax x1 -> x0, blocking collectives: 34.7 us -> none  [local(): peak_all = lax.pmax(maxima.astype(jnp.bfloat16), 'tok').astype(maxima.dtype)]
    psum x1 -> x0, blocking collectives: 34.5 us -> none  [local(): lax.psum(denom_terms.astype(jnp.bfloat16), 'tok').astype(jnp.float32)]
    reduce_sum x17 -> x0, other arithmetic: 8.03 us -> none  [the longest x8 4.42 us: attend_heads(): denoms.append(jnp.sum(weights, axis=1))]
    ppermute x4 -> x0, starting transfers between devices: 6.65 us -> none  [from_behind(): return lax.ppermute(block, axis, route)]
  transfers between devices with their start and end apart: 7 -> 0, of which waited for: 5 -> 0; matrix products, arithmetic and copies ran while one was open for 2% -> 0% of each run, Pallas kernels for 0% -> 0%
where the time goes in v1:
time: 114 us; the launch traced here: 112 us
  Pallas kernels  109 us (96%)
  local copies, waits for them, and re-layouts  3.21 us (3%)
    pallas_call x1, Pallas kernels, local_fused(): pl.pallas_call(functools.partial(window_kernel, n_tok, n_frame), out_shap...  109 us

profile of v1, /device:TPU:4, one launch (start us, length us, event | category | flops | bytes accessed | tf_op | source)
XLA Modules:
  0.0 112.3 jit_solution(8211251473947490766)
XLA Ops:
  0.0 1.3 %reshape.3.gain_ref = f32[3,1024]{1,0:T(4,128)} reshape(f32[3072]{0:T(1024)} %param.9) | data formatting | bytes 24576 | tf_op jit(solution)/shard_map/reshape | solution.py:489
  1.3 109.1 %shard_map.64 = f32[1,128,1024]{2,1,0:T(8,128)} custom-call(bf16[1,768,512]{2,1,0:T(8,128)(2,1)} %x_ref.1, bf16[512,2048]{1,0:T(8,128)(2,1)} %kvw_ref.1, bf16[128,1024]{1,0:T(8,128)(2,1)} %lq_ref.1, f32[3,1024]{1,0:T(4,128)} %reshape.3.gain_ref, bf16[3072,128]{1,0:T(8,128)(2,1)} %w_ref.1, bf16[1,128,1024]{2,1,0:T(8,128)(2,1)} %oq_ref.1), custom_call_target="tpu_custom_call" | custom-call | tf_op jit(solution)/shard_map/pallas_call | solution.py:480
  110.4 1.9 %copy.8 = f32[1,128,1024]{2,1,0:T(8,128)} copy(f32[1,128,1024]{2,1,0:T(8,128)} %shard_map.64) | data formatting | bytes 1048576

commit v2 on v1

--- a/solution.py
+++ b/solution.py
@@ -158,19 +158,21 @@
 def copy_ids(n_tok, pairs):
     names = []
     for j in range(1, pairs):
-        names += [("qz", j), ("qx", j), ("nz", j), ("sz", j), ("lz", j), ("lx", j)]
+        names += [("qz", j), ("qx", j)]
     for j in range(pairs):
-        names += [("nx", j), ("sx", j), ("t1", j), ("t2", j)]
+        names += [("t1", j), ("t2", j), ("mx", j)]
+        for g in range(2):
+            names += [(n, j, g) for n in ("nx", "sx", "nz", "sz", "lz", "fz")]
     for k in range(1, n_tok):
         names += [("qc", k), ("oq", k), ("out", k)]
-    names += [("qx", 0), ("lx", 0)]
+    names += [("qx", 0), ("wx",), ("wc",)]
     return {name: i for i, name in enumerate(names)}
 
 
 def window_kernel(
     n_tok, n_frame, x_ref, kvw_ref, lq_ref, gain_ref, w_ref, oq_ref, out_ref,
-    qbuf, kbuf, vbuf, w3, own_n, own_s, xs_n, xs_s, xr_n, xr_s, zs_n, zs_s, zr_n, zr_s,
-    lat, now, sq_own, ts1, ts2, tr1, tr2, mix_t, mix, oqbuf, osend, obuf, send_sem, recv_sem,
+    qbuf, kbuf, vbuf, wbuf, w3, own_n, own_s, xs_n, xs_s, xr_n, xr_s, zs_n, zs_s, zr_n, zr_s,
+    lat, now, sq_own, ts1, ts2, tr1, tr2, msend, mixbuf, mix_t, mix, oqbuf, osend, obuf, send_sem, recv_sem,
 ):
     heads = n_tok
     pairs = n_tok // 2
@@ -198,10 +200,10 @@
 
     peer = [flip(k) for k in range(n_tok)]
 
-    def copy(name, src, dst, where):
-        i = ids[name]
+    def copy(name, src, dst, where, send_name=None):
         return pltpu.make_async_remote_copy(
-            src_ref=src, dst_ref=dst, send_sem=send_sem.at[i], recv_sem=recv_sem.at[i],
+            src_ref=src, dst_ref=dst,
+            send_sem=send_sem.at[ids[send_name or name]], recv_sem=recv_sem.at[ids[name]],
             device_id=where, device_id_type=MESH,
         )
 
@@ -235,9 +237,6 @@
     for j in range(pairs - 1, 0, -1):
         send(("qz", j), own_half, qpart(2 * j, here), tok(2 * j))
     send(("qx", 0), own_half, qpart(1, here), tok(1))
-    for k in range(n_tok - 1, 0, -1):
-        cols = pl.ds(pl.multiple_of(peer[k] * dim, dim), dim)
-        send(("oq", k), oq_ref.at[0, :, cols], oqbuf.at[pl.ds(k * qrows, qrows), :], tok(k))
     qbuf[0:rows, :] = lq_ref[...]
     own_cols = pl.ds(pl.multiple_of(ti * dim, dim), dim)
     oqbuf[0:qrows, :] = oq_ref[0, :, own_cols]
@@ -245,7 +244,7 @@
     def project_keys(i, carry):
         cols = pl.ds(pl.multiple_of(i * 2 * dim, 2 * dim), 2 * dim)
         k = jnp.dot(x_ref[0], kvw_ref[:, cols], preferred_element_type=jnp.float32)
-        k = (k * factor).astype(jnp.bfloat16)
+        k = k.astype(jnp.bfloat16)
         kbuf[2 * i] = k[:, :dim]
         kbuf[2 * i + 1] = k[:, dim:]
         return carry
@@ -254,11 +253,6 @@
 
     arrived(("qx", 0), qpart(1, here), tok(1))
     send(("qc", 1), qpart(1, here), qpart(1, here), (sibling, ti))
-    for j in range(pairs - 1, 0, -1):
-        arrived(("qz", j), qpart(2 * j, here), tok(2 * j))
-        send(("qx", j), qpart(2 * j, here), qpart(2 * j + 1, here), tok(1))
-        send(("qc", 2 * j), qpart(2 * j, here), qpart(2 * j, here), (sibling, ti))
-
     def project_values(i, carry):
         cols = pl.ds(pl.multiple_of(width + i * 2 * dim, 2 * dim), 2 * dim)
         v = jnp.dot(x_ref[0], kvw_ref[:, cols], preferred_element_type=jnp.float32)
@@ -269,97 +263,157 @@
 
     lax.fori_loop(0, heads // 2, project_values, 0)
 
-    for j in range(pairs - 1, 0, -1):
-        k = 2 * j + 1
-        arrived(("qx", j), qpart(k, here), tok(1))
-        send(("qc", k), qpart(k, here), qpart(k, here), (sibling, ti))
-
-    for t in range(3):
-        w_t = w_ref[t * width : (t + 1) * width, :].T.astype(jnp.float32)
-        w3[t * dim : (t + 1) * dim, :] = (w_t * gain_ref[t : t + 1, :]).astype(jnp.bfloat16)
-
-    def merge_x(j):
-        arrived(("nx", j), xr_n.at[j], tok(1))
-        arrived(("sx", j), xr_s.at[j], tok(1))
-        m1, l1 = own_s[j, 0:heads, :], own_s[j, heads : 2 * heads, :]
-        m2, l2 = xr_s[j, 0:heads, :], xr_s[j, heads : 2 * heads, :]
+    group = heads // 2
+
+    def heads_of(g):
+        return pl.ds(g * group, group)
+
+    def merge_x(j, g):
+        arrived(("nx", j, g), xr_n.at[j, heads_of(g)], tok(1))
+        arrived(("sx", j, g), xr_s.at[j, g], tok(1))
+        m1, l1 = own_s[j, g, 0:group, :], own_s[j, g, group:, :]
+        m2, l2 = xr_s[j, g, 0:group, :], xr_s[j, g, group:, :]
         m = jnp.maximum(m1, m2)
         a1, a2 = jnp.exp2(m1 - m), jnp.exp2(m2 - m)
-        l = l1 * a1 + l2 * a2
-        if j == 0:
-            own_s[0, 0:heads, :] = m
-            own_s[0, heads : 2 * heads, :] = l
-        else:
-            zs_s[j, 0:heads, :] = m
-            zs_s[j, heads : 2 * heads, :] = l
-        for h in range(heads):
-            n = own_n[j, h] * a1[h : h + 1] + xr_n[j, h].astype(jnp.float32) * a2[h : h + 1]
+        target = own_s if j == 0 else zs_s
+        target[j, g, 0:group, :] = m
+        target[j, g, group:, :] = l1 * a1 + l2 * a2
+        for i in range(group):
+            h = g * group + i
+            n = own_n[j, h] * a1[i : i + 1] + xr_n[j, h].astype(jnp.float32) * a2[i : i + 1]
             if j == 0:
                 own_n[0, h] = n
             else:
                 zs_n[j, h] = n.astype(jnp.bfloat16)
         if j > 0:
-            send(("nz", j), zs_n.at[j], zr_n.at[j], tok(2 * j))
-            send(("sz", j), zs_s.at[j], zr_s.at[j], tok(2 * j))
-
-    for j in range(pairs - 1, -1, -1):
+            where = tok(2 * j)
+            send(("nz", j, g), zs_n.at[j, heads_of(g)], zr_n.at[j, heads_of(g)], where)
+            send(("sz", j, g), zs_s.at[j, g], zr_s.at[j, g], where)
+
+    def attend_unit(j, g):
+        def head_pair(i, carry):
+            for u in range(2):
+                r = 2 * i + u
+                h = g * group + r
+                cols = pl.ds(pl.multiple_of(h * dim, dim), dim)
+                q = qbuf[2 * j * rows : (2 * j + 2) * rows, cols]
+                n, m, l = attend_columns(kbuf[h], vbuf[h], q, factor)
+                own_n[j, h] = n[:, :rows]
+                own_s[j, g, pl.ds(r, 1), :] = m[:, :rows]
+                own_s[j, g, pl.ds(group + r, 1), :] = l[:, :rows]
+                xs_n[j, h] = n[:, rows:].astype(jnp.bfloat16)
+                xs_s[j, g, pl.ds(r, 1), :] = m[:, rows:]
+                xs_s[j, g, pl.ds(group + r, 1), :] = l[:, rows:]
+            return carry
+
+        lax.fori_loop(0, group // 2, head_pair, 0)
+        send(("nx", j, g), xs_n.at[j, heads_of(g)], xr_n.at[j, heads_of(g)], tok(1))
+        send(("sx", j, g), xs_s.at[j, g], xr_s.at[j, g], tok(1))
+
+    def wait_queries(j):
         for k in (2 * j, 2 * j + 1):
             if k > 0:
                 arrived(("qc", k), qpart(k, there), (sibling, ti))
 
-        def head_pair(i, carry, j=j):
-            for u in range(2):
-                h = 2 * i + u
-                cols = pl.ds(pl.multiple_of(h * dim, dim), dim)
-                q = qbuf[2 * j * rows : (2 * j + 2) * rows, cols]
-                n, m, l = attend_columns(kbuf[h], vbuf[h], q, None)
-                own_n[j, h] = n[:, :rows]
-                own_s[j, pl.ds(h, 1), :] = m[:, :rows]
-                own_s[j, pl.ds(heads + h, 1), :] = l[:, :rows]
-                xs_n[j, h] = n[:, rows:].astype(jnp.bfloat16)
-                xs_s[j, pl.ds(h, 1), :] = m[:, rows:]
-                xs_s[j, pl.ds(heads + h, 1), :] = l[:, rows:]
-            return carry
-
-        lax.fori_loop(0, heads // 2, head_pair, 0)
-        send(("nx", j), xs_n.at[j], xr_n.at[j], tok(1))
-        send(("sx", j), xs_s.at[j], xr_s.at[j], tok(1))
-        if j < pairs - 1:
-            merge_x(j + 1)
-    merge_x(0)
-
+    wait_queries(0)
+    attend_unit(0, 0)
     for j in range(pairs - 1, 0, -1):
-        arrived(("nz", j), zr_n.at[j], tok(2 * j))
-        arrived(("sz", j), zr_s.at[j], tok(2 * j))
-    peaks = [own_s[0, 0:heads, :]] + [zr_s[j, 0:heads, :] for j in range(1, pairs)]
-    dens = [own_s[0, heads : 2 * heads, :]]
-    dens += [zr_s[j, heads : 2 * heads, :] for j in range(1, pairs)]
-    top = functools.reduce(jnp.maximum, peaks)
-    scale = [jnp.exp2(p - top) for p in peaks]
-    total = sum(d * s for d, s in zip(dens, scale))
-    scale = [s / total for s in scale]
-    for h in range(heads):
-        n = own_n[0, h] * scale[0][h : h + 1]
-        for j in range(1, pairs):
-            n = n + zr_n[j, h].astype(jnp.float32) * scale[j][h : h + 1]
-        lat[0, h * dim : (h + 1) * dim, :] = n.astype(jnp.bfloat16)
-
+        arrived(("qz", j), qpart(2 * j, here), tok(2 * j))
+        send(("qx", j), qpart(2 * j, here), qpart(2 * j + 1, here), tok(1))
+        send(("qc", 2 * j), qpart(2 * j, here), qpart(2 * j, here), (sibling, ti))
+    attend_unit(0, 1)
+    merge_x(0, 0)
     for j in range(pairs - 1, 0, -1):
-        send(("lz", j), lat.at[0], lat.at[2 * j], tok(2 * j))
-    send(("lx", 0), lat.at[0], lat.at[1], tok(1))
-
-    def mix_pair(c):
-        both = jnp.concatenate([lat[2 * c], lat[2 * c + 1]], axis=1)
-        wide = both.astype(jnp.float32)
+        k = 2 * j + 1
+        arrived(("qx", j), qpart(k, here), tok(1))
+        send(("qc", k), qpart(k, here), qpart(k, here), (sibling, ti))
+    for k in range(n_tok - 1, 0, -1):
+        cols = pl.ds(pl.multiple_of(peer[k] * dim, dim), dim)
+        send(("oq", k), oq_ref.at[0, :, cols], oqbuf.at[pl.ds(k * qrows, qrows), :], tok(k))
+    before = (0, 1)
+    for j in range(pairs - 1, 0, -1):
+        wait_queries(j)
+        for g in range(2):
+            attend_unit(j, g)
+            merge_x(*before)
+            before = (j, g)
+    w_rows = w_ref.shape[0] // 2
+    w_here = pl.ds(pl.multiple_of(mine * w_rows, w_rows), w_rows)
+    w_there = pl.ds(pl.multiple_of((1 - mine) * w_rows, w_rows), w_rows)
+    send(("wx",), w_ref.at[w_here, :], wbuf.at[w_here, :], tok(1))
+    merge_x(*before)
+
+    line = lax.div(ti, 2)
+    middle = jnp.logical_and(line > 0, line < pairs - 1)
+
+    def lat_part(slot, g):
+        return lat.at[slot, pl.ds(g * group * dim, group * dim), :]
+
+    def forward(slot, g):
+        far, near = tok(2 * (pairs - 1)), tok(2)
+        plan = {0: (3, far), 1: (2, far), 3: (2, near), 2: (3, near)}
+        there_slot, where = plan[slot]
+        return copy(
+            ("lz", there_slot, g), lat_part(slot, g), lat_part(there_slot, g), where, ("fz", slot, g)
+        )
+
+    def pass_on(slot):
+        for g in range(2):
+            arrived(("lz", slot, g), lat_part(slot, g), tok(2))
+            forward(slot, g).start()
+
+    for g in range(2):
+        for j in range(pairs - 1, 0, -1):
+            arrived(("nz", j, g), zr_n.at[j, heads_of(g)], tok(2 * j))
+            arrived(("sz", j, g), zr_s.at[j, g], tok(2 * j))
+        peaks = [own_s[0, g, 0:group, :]] + [zr_s[j, g, 0:group, :] for j in range(1, pairs)]
+        dens = [own_s[0, g, group:, :]] + [zr_s[j, g, group:, :] for j in range(1, pairs)]
+        top = functools.reduce(jnp.maximum, peaks)
+        scale = [jnp.exp2(p - top) for p in peaks]
+        total = sum(d * s for d, s in zip(dens, scale))
+        scale = [s / total for s in scale]
+        for i in range(group):
+            h = g * group + i
+            n = own_n[0, h] * scale[0][i : i + 1]
+            for j in range(1, pairs):
+                n = n + zr_n[j, h].astype(jnp.float32) * scale[j][i : i + 1]
+            lat[0, h * dim : (h + 1) * dim, :] = n.astype(jnp.bfloat16)
+        send(("lz", 1, g), lat_part(0, g), lat_part(1, g), tok(2))
+
+        @pl.when(middle)
+        def _():
+            forward(0, g).start()
+
+    def mix_weights(source, place):
+        for t in range(3):
+            w_t = source[t * width : (t + 1) * width, :].T.astype(jnp.float32)
+            gain = gain_ref[t * width : (t + 1) * width].reshape(1, width)
+            at = 2 * t + place
+            w3[at * dim : (at + 1) * dim, :] = (w_t * gain).astype(jnp.bfloat16)
+
+    arrived(("wx",), wbuf.at[w_here, :], tok(1))
+    send(("wc",), wbuf.at[w_here, :], wbuf.at[w_here, :], (sibling, ti))
+    mix_weights(w_ref, 0)
+
+    @pl.when(middle)
+    def _():
+        pass_on(1)
+
+    arrived(("wc",), wbuf.at[w_there, :], (sibling, ti))
+    mix_weights(wbuf, 1)
+
+    def mix_rows(c):
+        block = lat[c]
+        wide = block.astype(jnp.float32)
         squares = jnp.sum(wide * wide, axis=0, keepdims=True)
-        terms = jnp.dot(w3[...], both, preferred_element_type=jnp.float32)
-        now[c] = terms[:dim]
+        terms = jnp.dot(w3[...], block, preferred_element_type=jnp.float32)
+        now[c] = terms[: 2 * dim]
         sq_own[c] = jnp.broadcast_to(squares, sq_own.shape[1:])
-        sq = jnp.broadcast_to(squares, (16, 2 * rows)).astype(jnp.bfloat16)
-        ts1[c, 0:dim, :] = terms[dim : 2 * dim].astype(jnp.bfloat16)
-        ts1[c, dim : dim + 16, :] = sq
-        ts2[c, 0:dim, :] = terms[2 * dim :].astype(jnp.bfloat16)
-        ts2[c, dim : dim + 16, :] = sq
+        sq = jnp.broadcast_to(squares, (16, rows)).astype(jnp.bfloat16)
+        ts1[c, 0 : 2 * dim, :] = terms[2 * dim : 4 * dim].astype(jnp.bfloat16)
+        ts1[c, 2 * dim :, :] = sq
+        ts2[c, 0 : 2 * dim, :] = terms[4 * dim :].astype(jnp.bfloat16)
+        ts2[c, 2 * dim :, :] = sq
 
         @pl.when(fi < n_frame - 1)
         def _():
@@ -369,14 +423,6 @@
         def _():
             copy(("t2", c), ts2.at[c], tr2.at[c], (lax.rem(fi + 2, n_frame), ti)).start()
 
-    order = [1, 2, 3] if pairs == 4 else list(range(1, pairs))
-    for j in order:
-        arrived(("lz", j), lat.at[2 * j], tok(2 * j))
-        send(("lx", j), lat.at[2 * j], lat.at[2 * j + 1], tok(1))
-    for c in [0] + order:
-        arrived(("lx", c), lat.at[2 * c + 1], tok(1))
-        mix_pair(c)
-
     @pl.when(fi < 1)
     def _():
         tr1[...] = jnp.zeros_like(tr1)
@@ -385,8 +431,7 @@
     def _():
         tr2[...] = jnp.zeros_like(tr2)
 
-    for c in [0] + order:
-
+    def finish_rows(c):
         @pl.when(fi >= 1)
         def _():
             copy(("t1", c), ts1.at[c], tr1.at[c], (lax.rem(fi + 1, n_frame), ti)).wait_recv()
@@ -395,16 +440,55 @@
         def _():
             copy(("t2", c), ts2.at[c], tr2.at[c], (lax.rem(fi + 2, n_frame), ti)).wait_recv()
 
-        summed = now[c] + tr1[c, 0:dim, :].astype(jnp.float32) + tr2[c, 0:dim, :].astype(jnp.float32)
-        squares = (
-            sq_own[c, 0:1, :]
-            + tr1[c, dim : dim + 16, :].astype(jnp.float32)[0:1]
-            + tr2[c, dim : dim + 16, :].astype(jnp.float32)[0:1]
-        )
+        before_one = tr1[c].astype(jnp.float32)
+        before_two = tr2[c].astype(jnp.float32)
+        summed = now[c] + before_one[: 2 * dim] + before_two[: 2 * dim]
+        squares = sq_own[c, 0:1, :] + before_one[2 * dim : 2 * dim + 1] + before_two[2 * dim : 2 * dim + 1]
         z = summed * lax.rsqrt(squares / (3 * width) + 1e-06)
         mixed = (0.5 * z * (1.0 + lax.erf(z * math.sqrt(0.5)))).astype(jnp.bfloat16)
-        mix_t[:, c * 2 * rows : (c + 1) * 2 * rows] = mixed
-        mix[c * 2 * rows : (c + 1) * 2 * rows, :] = mixed.T
+        msend[c] = mixed[dim:]
+        send(("mx", c), msend.at[c], mixbuf.at[2 * c + 1], tok(1))
+        mixbuf[2 * c] = mixed[:dim]
+
+    @pl.when(middle)
+    def _():
+        pass_on(3)
+
+    mix_rows(0)
+
+    @pl.when(middle)
+    def _():
+        pass_on(2)
+
+    @pl.when(jnp.logical_not(middle))
+    def _():
+        for g in range(2):
+            arrived(("lz", 1, g), lat_part(1, g), tok(2))
+
+    mix_rows(1)
+
+    @pl.when(jnp.logical_not(middle))
+    def _():
+        for g in range(2):
+            arrived(("lz", 2, g), lat_part(2, g), tok(2))
+
+    finish_rows(0)
+    mix_rows(2)
+
+    @pl.when(jnp.logical_not(middle))
+    def _():
+        for g in range(2):
+            arrived(("lz", 3, g), lat_part(3, g), tok(2))
+
+    mix_rows(3)
+    for c in range(1, pairs):
+        finish_rows(c)
+    for k in range(n_tok):
+        if k % 2:
+            arrived(("mx", k // 2), mixbuf.at[k], tok(1))
+        block = mixbuf[k]
+        mix_t[:, k * rows : (k + 1) * rows] = block
+        mix[k * rows : (k + 1) * rows, :] = block.T
 
     for k in range(1, n_tok):
         arrived(("oq", k), oqbuf.at[pl.ds(k * qrows, qrows), :], tok(k))
@@ -426,6 +510,13 @@
 
     for c in started:
         c.wait_send()
+
+    @pl.when(middle)
+    def _():
+        for g in range(2):
+            for slot in range(pairs):
+                forward(slot, g).wait_send()
+
     for c in range(pairs):
 
         @pl.when(fi < n_frame - 1)
@@ -448,7 +539,7 @@
     rows = latent_queries.shape[0]
     qrows = output_queries.shape[1]
     bf16, f32 = jnp.bfloat16, jnp.float32
-    stats = (pairs, 2 * heads, rows)
+    stats = (pairs, 2, heads, rows)
     block = (pairs, heads, dim, rows)
     n_ids = len(copy_ids(n_tok, pairs))
     vmem = pltpu.VMEM
@@ -456,19 +547,22 @@
         vmem((n_tok * rows, width), bf16),
         vmem((heads, n_in, dim), bf16),
         vmem((heads, dim, n_in), bf16),
-        vmem((3 * dim, width), bf16),
+        vmem((3 * width, dim), bf16),
+        vmem((6 * dim, width), bf16),
         vmem(block, f32), vmem(stats, f32),
         vmem(block, bf16), vmem(stats, f32),
         vmem(block, bf16), vmem(stats, f32),
         vmem(block, bf16), vmem(stats, f32),
         vmem(block, bf16), vmem(stats, f32),
-        vmem((n_tok, width, rows), bf16),
-        vmem((pairs, dim, 2 * rows), f32),
-        vmem((pairs, 8, 2 * rows), f32),
-        vmem((pairs, dim + 16, 2 * rows), bf16),
-        vmem((pairs, dim + 16, 2 * rows), bf16),
-        vmem((pairs, dim + 16, 2 * rows), bf16),
-        vmem((pairs, dim + 16, 2 * rows), bf16),
+        vmem((pairs, width, rows), bf16),
+        vmem((pairs, 2 * dim, rows), f32),
+        vmem((pairs, 8, rows), f32),
+        vmem((pairs, 2 * dim + 16, rows), bf16),
+        vmem((pairs, 2 * dim + 16, rows), bf16),
+        vmem((pairs, 2 * dim + 16, rows), bf16),
+        vmem((pairs, 2 * dim + 16, rows), bf16),
+        vmem((pairs, dim, rows), bf16),
+        vmem((n_tok, dim, rows), bf16),
         vmem((dim, n_tok * rows), bf16),
         vmem((n_tok * rows, dim), bf16),
         vmem((n_tok * qrows, dim), bf16),
@@ -486,7 +580,7 @@
         compiler_params=pltpu.CompilerParams(
             collective_id=0, has_side_effects=True, vmem_limit_bytes=56 * 1024 * 1024
         ),
-    )(inputs, kv_weight, latent_queries, mix_gain.reshape(3, width), mix_weight, output_queries)
+    )(inputs, kv_weight, latent_queries, mix_gain, mix_weight, output_queries)
 
 
 def pick_local(mesh):

time: 114 us -> 98.8 us (0.87); the launches traced: 112 us -> 98.6 us
  Pallas kernels: 109 us -> 96.7 us
  local copies, waits for them, and re-layouts: 3.21 us -> 1.89 us
    pallas_call x1, Pallas kernels: 109 us -> 96.7 us  [local_fused(): pl.pallas_call(functools.partial(window_kernel, n_tok, n_frame), out_shap...]
    reshape x1 -> x0, local copies, waits for them, and re-layouts: 1.32 us -> none  [local_fused(): mix_gain.reshape(3, width)]
where the time goes in v2:
time: 98.8 us; the launch traced here: 98.6 us
  Pallas kernels  96.7 us (98%)
  local copies, waits for them, and re-layouts  1.89 us (2%)
    pallas_call x1, Pallas kernels, local_fused(): pl.pallas_call(functools.partial(window_kernel, n_tok, n_frame), out_shap...  96.7 us

profile of v2, /device:TPU:4, one launch (start us, length us, event | category | flops | bytes accessed | tf_op | source)
XLA Modules:
  0.0 98.6 jit_solution(15561539501276210313)
XLA Ops:
  0.0 96.7 %shard_map.64 = f32[1,128,1024]{2,1,0:T(8,128)} custom-call(bf16[1,768,512]{2,1,0:T(8,128)(2,1)} %x_ref.1, bf16[512,2048]{1,0:T(8,128)(2,1)} %kvw_ref.1, bf16[128,1024]{1,0:T(8,128)(2,1)} %lq_ref.1, f32[3072]{0:T(1024)} %gain_ref.1, bf16[3072,128]{1,0:T(8,128)(2,1)} %w_ref.1, bf16[1,128,1024]{2,1,0:T(8,128)(2,1)} %oq_ref.1), custom_call_target="tpu_custom_call" | custom-call | tf_op jit(solution)/shard_map/pallas_call | solution.py:574
  96.7 1.9 %copy.8 = f32[1,128,1024]{2,1,0:T(8,128)} copy(f32[1,128,1024]{2,1,0:T(8,128)} %shard_map.64) | data formatting | bytes 1048576

commit v3 on v2

--- a/solution.py
+++ b/solution.py
@@ -138,21 +138,30 @@
 
 MESH = pl.DeviceIdType.MESH
 LOG2E = 1.4426950408889634
+ONES = 16
 
 
 def dot_nt(a, b):
     return lax.dot_general(a, b, (((1,), (1,)), ((), ())), preferred_element_type=jnp.float32)
 
 
-def attend_columns(keys, values_t, queries, factor):
-    scores = dot_nt(keys, queries)
-    if factor is not None:
-        scores = scores * factor
-    peak = jnp.max(scores, axis=0, keepdims=True)
-    weights = jnp.exp2(scores - peak)
-    denom = jnp.sum(weights, axis=0, keepdims=True)
-    numer = jnp.dot(values_t, weights.astype(jnp.bfloat16), preferred_element_type=jnp.float32)
-    return numer, peak, denom
+def attend_units(units, finish):
+    def score(unit):
+        keys, _, queries, factor = unit()
+        scores = dot_nt(keys, queries)
+        return scores if factor is None else scores * factor
+
+    ahead = score(units[0])
+    for i, unit in enumerate(units):
+        scores = ahead
+        if i + 1 < len(units):
+            ahead = score(units[i + 1])
+        peak = jnp.max(scores, axis=0, keepdims=True)
+        weights = jnp.exp2(scores - peak).astype(jnp.bfloat16)
+        values = unit()[1]
+        numer = jnp.dot(values, weights, preferred_element_type=jnp.float32)
+        dim = values.shape[0] - ONES
+        finish(i, numer[:dim], peak, numer[dim : dim + 1])
 
 
 def copy_ids(n_tok, pairs):
@@ -244,12 +253,12 @@
     def project_keys(i, carry):
         cols = pl.ds(pl.multiple_of(i * 2 * dim, 2 * dim), 2 * dim)
         k = jnp.dot(x_ref[0], kvw_ref[:, cols], preferred_element_type=jnp.float32)
-        k = k.astype(jnp.bfloat16)
+        k = (k * factor).astype(jnp.bfloat16)
         kbuf[2 * i] = k[:, :dim]
         kbuf[2 * i + 1] = k[:, dim:]
         return carry
 
-    lax.fori_loop(0, heads // 2, project_keys, 0)
+    lax.fori_loop(0, heads // 2, project_keys, 0, unroll=True)
 
     arrived(("qx", 0), qpart(1, here), tok(1))
     send(("qc", 1), qpart(1, here), qpart(1, here), (sibling, ti))
@@ -257,11 +266,12 @@
         cols = pl.ds(pl.multiple_of(width + i * 2 * dim, 2 * dim), 2 * dim)
         v = jnp.dot(x_ref[0], kvw_ref[:, cols], preferred_element_type=jnp.float32)
         v = v.astype(jnp.bfloat16).T
-        vbuf[2 * i] = v[:dim]
-        vbuf[2 * i + 1] = v[dim:]
+        vbuf[2 * i, 0:dim, :] = v[:dim]
+        vbuf[2 * i + 1, 0:dim, :] = v[dim:]
         return carry
 
-    lax.fori_loop(0, heads // 2, project_values, 0)
+    vbuf[:, dim:, :] = jnp.ones((heads, ONES, vbuf.shape[2]), jnp.bfloat16)
+    lax.fori_loop(0, heads // 2, project_values, 0, unroll=True)
 
     group = heads // 2
 
@@ -291,22 +301,21 @@
             send(("sz", j, g), zs_s.at[j, g], zr_s.at[j, g], where)
 
     def attend_unit(j, g):
-        def head_pair(i, carry):
-            for u in range(2):
-                r = 2 * i + u
-                h = g * group + r
-                cols = pl.ds(pl.multiple_of(h * dim, dim), dim)
-                q = qbuf[2 * j * rows : (2 * j + 2) * rows, cols]
-                n, m, l = attend_columns(kbuf[h], vbuf[h], q, factor)
-                own_n[j, h] = n[:, :rows]
-                own_s[j, g, pl.ds(r, 1), :] = m[:, :rows]
-                own_s[j, g, pl.ds(group + r, 1), :] = l[:, :rows]
-                xs_n[j, h] = n[:, rows:].astype(jnp.bfloat16)
-                xs_s[j, g, pl.ds(r, 1), :] = m[:, rows:]
-                xs_s[j, g, pl.ds(group + r, 1), :] = l[:, rows:]
-            return carry
-
-        lax.fori_loop(0, group // 2, head_pair, 0)
+        def unit(r):
+            h = g * group + r
+            q = qbuf[2 * j * rows : (2 * j + 2) * rows, h * dim : (h + 1) * dim]
+            return kbuf[h], vbuf[h], q, None
+
+        def finish(r, n, m, l):
+            h = g * group + r
+            own_n[j, h] = n[:, :rows]
+            own_s[j, g, r : r + 1, :] = m[:, :rows]
+            own_s[j, g, group + r : group + r + 1, :] = l[:, :rows]
+            xs_n[j, h] = n[:, rows:].astype(jnp.bfloat16)
+            xs_s[j, g, r : r + 1, :] = m[:, rows:]
+            xs_s[j, g, group + r : group + r + 1, :] = l[:, rows:]
+
+        attend_units([functools.partial(unit, r) for r in range(group)], finish)
         send(("nx", j, g), xs_n.at[j, heads_of(g)], xr_n.at[j, heads_of(g)], tok(1))
         send(("sx", j, g), xs_s.at[j, g], xr_s.at[j, g], tok(1))
 
@@ -487,14 +496,19 @@
         if k % 2:
             arrived(("mx", k // 2), mixbuf.at[k], tok(1))
         block = mixbuf[k]
-        mix_t[:, k * rows : (k + 1) * rows] = block
+        mix_t[0:dim, k * rows : (k + 1) * rows] = block
         mix[k * rows : (k + 1) * rows, :] = block.T
 
     for k in range(1, n_tok):
         arrived(("oq", k), oqbuf.at[pl.ds(k * qrows, qrows), :], tok(k))
-    for c in range(pairs - 1, -1, -1):
-        q = oqbuf[2 * c * qrows : (2 * c + 2) * qrows, :]
-        n, m, l = attend_columns(mix[...], mix_t[...], q, factor)
+    mix_t[dim:, :] = jnp.ones((ONES, mix_t.shape[1]), jnp.bfloat16)
+
+    def decode_unit(i):
+        c = pairs - 1 - i
+        return mix[...], mix_t[...], oqbuf[2 * c * qrows : (2 * c + 2) * qrows, :], factor
+
+    def decode_finish(i, n, m, l):
+        c = pairs - 1 - i
         o = (n / l).T
         for k in (2 * c, 2 * c + 1):
             part = o[(k - 2 * c) * qrows : (k - 2 * c + 1) * qrows]
@@ -503,6 +517,8 @@
             else:
                 osend[k] = part.astype(jnp.bfloat16)
                 send(("out", k), osend.at[k], obuf.at[k], tok(k))
+
+    attend_units([functools.partial(decode_unit, i) for i in range(pairs)], decode_finish)
     for k in range(n_tok - 1, 0, -1):
         arrived(("out", k), obuf.at[k], tok(k))
         cols = pl.ds(pl.multiple_of(peer[k] * dim, dim), dim)
@@ -546,7 +562,7 @@
     scratch = [
         vmem((n_tok * rows, width), bf16),
         vmem((heads, n_in, dim), bf16),
-        vmem((heads, dim, n_in), bf16),
+        vmem((heads, dim + ONES, n_in), bf16),
         vmem((3 * width, dim), bf16),
         vmem((6 * dim, width), bf16),
         vmem(block, f32), vmem(stats, f32),
@@ -563,7 +579,7 @@
         vmem((pairs, 2 * dim + 16, rows), bf16),
         vmem((pairs, dim, rows), bf16),
         vmem((n_tok, dim, rows), bf16),
-        vmem((dim, n_tok * rows), bf16),
+        vmem((dim + ONES, n_tok * rows), bf16),
         vmem((n_tok * rows, dim), bf16),
         vmem((n_tok * qrows, dim), bf16),
         vmem((n_tok, qrows, dim), bf16),

time: 98.8 us -> 95.6 us (0.968)
  Pallas kernels: 96.7 us -> 93.2 us
    pallas_call x1, Pallas kernels: 96.7 us -> 93.2 us  [local_fused(): pl.pallas_call(functools.partial(window_kernel, n_tok, n_frame), out_shap...]
where the time goes in v3:
time: 95.6 us; the launch traced here: 95.1 us
  Pallas kernels  93.2 us (97%)
  local copies, waits for them, and re-layouts  1.89 us (2%)
    pallas_call x1, Pallas kernels, local_fused(): pl.pallas_call(functools.partial(window_kernel, n_tok, n_frame), out_shap...  93.2 us

profile of v3, /device:TPU:4, one launch (start us, length us, event | category | flops | bytes accessed | tf_op | source)
XLA Modules:
  0.0 95.1 jit_solution(12218286907693274960)
XLA Ops:
  0.0 93.2 %shard_map.64 = f32[1,128,1024]{2,1,0:T(8,128)} custom-call(bf16[1,768,512]{2,1,0:T(8,128)(2,1)} %x_ref.1, bf16[512,2048]{1,0:T(8,128)(2,1)} %kvw_ref.1, bf16[128,1024]{1,0:T(8,128)(2,1)} %lq_ref.1, f32[3072]{0:T(1024)} %gain_ref.1, bf16[3072,128]{1,0:T(8,128)(2,1)} %w_ref.1, bf16[1,128,1024]{2,1,0:T(8,128)(2,1)} %oq_ref.1), custom_call_target="tpu_custom_call" | custom-call | tf_op jit(solution)/shard_map/pallas_call | solution.py:590
  93.2 1.9 %copy.8 = f32[1,128,1024]{2,1,0:T(8,128)} copy(f32[1,128,1024]{2,1,0:T(8,128)} %shard_map.64) | data formatting | bytes 1048576

commit v4 on v3

--- a/solution.py
+++ b/solution.py
@@ -173,7 +173,7 @@
         for g in range(2):
             names += [(n, j, g) for n in ("nx", "sx", "nz", "sz", "lz", "fz")]
     for k in range(1, n_tok):
-        names += [("qc", k), ("oq", k), ("out", k)]
+        names += [("qc", k), ("qy", k), ("oq", k), ("out", k)]
     names += [("qx", 0), ("wx",), ("wc",)]
     return {name: i for i, name in enumerate(names)}
 
@@ -239,13 +239,29 @@
     here = pl.multiple_of(mine * half, half)
     there = pl.multiple_of((1 - mine) * half, half)
 
-    def qpart(k, off):
-        return qbuf.at[pl.ds(k * rows + off, half), :]
-
-    own_half = lq_ref.at[pl.ds(here, half), :]
+    quarter = half // 2
+    plane = lax.rem(lax.div(fi, 2), 2)
+    across = fi + 2 - 4 * plane
+    near_rows = pl.multiple_of(here + plane * quarter, quarter)
+    far_rows = pl.multiple_of(here + (1 - plane) * quarter, quarter)
+
+    def qpart(k, off, count=half):
+        return qbuf.at[pl.ds(k * rows + off, count), :]
+
+    def qnear(k):
+        return qpart(k, near_rows, quarter)
+
+    def send_across(k):
+        send(("qy", k), qnear(k), qnear(k), (across, ti))
+
+    def send_sibling(k):
+        arrived(("qy", k), qpart(k, far_rows, quarter), (across, ti))
+        send(("qc", k), qpart(k, here), qpart(k, here), (sibling, ti))
+
+    own_part = lq_ref.at[pl.ds(near_rows, quarter), :]
     for j in range(pairs - 1, 0, -1):
-        send(("qz", j), own_half, qpart(2 * j, here), tok(2 * j))
-    send(("qx", 0), own_half, qpart(1, here), tok(1))
+        send(("qz", j), own_part, qnear(2 * j), tok(2 * j))
+    send(("qx", 0), own_part, qnear(1), tok(1))
     qbuf[0:rows, :] = lq_ref[...]
     own_cols = pl.ds(pl.multiple_of(ti * dim, dim), dim)
     oqbuf[0:qrows, :] = oq_ref[0, :, own_cols]
@@ -260,8 +276,8 @@
 
     lax.fori_loop(0, heads // 2, project_keys, 0, unroll=True)
 
-    arrived(("qx", 0), qpart(1, here), tok(1))
-    send(("qc", 1), qpart(1, here), qpart(1, here), (sibling, ti))
+    arrived(("qx", 0), qnear(1), tok(1))
+    send_across(1)
     def project_values(i, carry):
         cols = pl.ds(pl.multiple_of(width + i * 2 * dim, 2 * dim), 2 * dim)
         v = jnp.dot(x_ref[0], kvw_ref[:, cols], preferred_element_type=jnp.float32)
@@ -324,18 +340,21 @@
             if k > 0:
                 arrived(("qc", k), qpart(k, there), (sibling, ti))
 
+    send_sibling(1)
+    for j in range(pairs - 1, 0, -1):
+        arrived(("qz", j), qnear(2 * j), tok(2 * j))
+        send(("qx", j), qnear(2 * j), qnear(2 * j + 1), tok(1))
+        send_across(2 * j)
     wait_queries(0)
     attend_unit(0, 0)
     for j in range(pairs - 1, 0, -1):
-        arrived(("qz", j), qpart(2 * j, here), tok(2 * j))
-        send(("qx", j), qpart(2 * j, here), qpart(2 * j + 1, here), tok(1))
-        send(("qc", 2 * j), qpart(2 * j, here), qpart(2 * j, here), (sibling, ti))
+        arrived(("qx", j), qnear(2 * j + 1), tok(1))
+        send_across(2 * j + 1)
+        send_sibling(2 * j)
     attend_unit(0, 1)
+    for j in range(pairs - 1, 0, -1):
+        send_sibling(2 * j + 1)
     merge_x(0, 0)
-    for j in range(pairs - 1, 0, -1):
-        k = 2 * j + 1
-        arrived(("qx", j), qpart(k, here), tok(1))
-        send(("qc", k), qpart(k, here), qpart(k, here), (sibling, ti))
     for k in range(n_tok - 1, 0, -1):
         cols = pl.ds(pl.multiple_of(peer[k] * dim, dim), dim)
         send(("oq", k), oq_ref.at[0, :, cols], oqbuf.at[pl.ds(k * qrows, qrows), :], tok(k))
@@ -601,7 +620,7 @@
 
 def pick_local(mesh):
     n_tok, n_frame = mesh.shape["tok"], mesh.shape["frame"]
-    fits = n_tok == HEADS and n_frame % 2 == 0 and n_frame > 2
+    fits = n_tok == HEADS and n_frame % 4 == 0
     return local_fused if fits else local
 
 

time: 95.6 us -> 91 us (0.952)
  Pallas kernels: 93.2 us -> 88.5 us
    pallas_call x1, Pallas kernels: 93.2 us -> 88.5 us  [local_fused(): pl.pallas_call(functools.partial(window_kernel, n_tok, n_frame), out_shap...]
where the time goes in v4:
time: 91 us; the launch traced here: 90.4 us
  Pallas kernels  88.5 us (97%)
  local copies, waits for them, and re-layouts  1.89 us (2%)
    pallas_call x1, Pallas kernels, local_fused(): pl.pallas_call(functools.partial(window_kernel, n_tok, n_frame), out_shap...  88.5 us
    unnamed x1, local copies, waits for them, and re-layouts  1.89 us

profile of v4, /device:TPU:4, one launch (start us, length us, event | category | flops | bytes accessed | tf_op | source)
XLA Modules:
  0.0 90.4 jit_solution(7676266057492587953)
XLA Ops:
  0.0 88.5 %shard_map.64 = f32[1,128,1024]{2,1,0:T(8,128)} custom-call(bf16[1,768,512]{2,1,0:T(8,128)(2,1)} %x_ref.1, bf16[512,2048]{1,0:T(8,128)(2,1)} %kvw_ref.1, bf16[128,1024]{1,0:T(8,128)(2,1)} %lq_ref.1, f32[3072]{0:T(1024)} %gain_ref.1, bf16[3072,128]{1,0:T(8,128)(2,1)} %w_ref.1, bf16[1,128,1024]{2,1,0:T(8,128)(2,1)} %oq_ref.1), custom_call_target="tpu_custom_call" | custom-call | tf_op jit(solution)/shard_map/pallas_call | solution.py:609
  88.6 1.9 %copy.8 = f32[1,128,1024]{2,1,0:T(8,128)} copy(f32[1,128,1024]{2,1,0:T(8,128)} %shard_map.64) | data formatting | bytes 1048576

commit v5 on v4

--- a/solution.py
+++ b/solution.py
@@ -181,7 +181,7 @@
 def window_kernel(
     n_tok, n_frame, x_ref, kvw_ref, lq_ref, gain_ref, w_ref, oq_ref, out_ref,
     qbuf, kbuf, vbuf, wbuf, w3, own_n, own_s, xs_n, xs_s, xr_n, xr_s, zs_n, zs_s, zr_n, zr_s,
-    lat, now, sq_own, ts1, ts2, tr1, tr2, msend, mixbuf, mix_t, mix, oqbuf, osend, obuf, send_sem, recv_sem,
+    lat, now, sq_own, ts1, ts2, tr1, tr2, msend, mixbuf, mix_t, mix, oqbuf, dec_n, dec_s, osend, obuf, send_sem, recv_sem,
 ):
     heads = n_tok
     pairs = n_tok // 2
@@ -390,6 +390,15 @@
             arrived(("lz", slot, g), lat_part(slot, g), tok(2))
             forward(slot, g).start()
 
+    def mix_weights(source, place):
+        for t in range(3):
+            w_t = source[t * width : (t + 1) * width, :].T.astype(jnp.float32)
+            gain = gain_ref[t * width : (t + 1) * width].reshape(1, width)
+            at = 2 * t + place
+            w3[at * dim : (at + 1) * dim, :] = (w_t * gain).astype(jnp.bfloat16)
+
+    mix_weights(w_ref, 0)
+
     for g in range(2):
         for j in range(pairs - 1, 0, -1):
             arrived(("nz", j, g), zr_n.at[j, heads_of(g)], tok(2 * j))
@@ -412,16 +421,8 @@
         def _():
             forward(0, g).start()
 
-    def mix_weights(source, place):
-        for t in range(3):
-            w_t = source[t * width : (t + 1) * width, :].T.astype(jnp.float32)
-            gain = gain_ref[t * width : (t + 1) * width].reshape(1, width)
-            at = 2 * t + place
-            w3[at * dim : (at + 1) * dim, :] = (w_t * gain).astype(jnp.bfloat16)
-
     arrived(("wx",), wbuf.at[w_here, :], tok(1))
     send(("wc",), wbuf.at[w_here, :], wbuf.at[w_here, :], (sibling, ti))
-    mix_weights(w_ref, 0)
 
     @pl.when(middle)
     def _():
@@ -478,6 +479,49 @@
         send(("mx", c), msend.at[c], mixbuf.at[2 * c + 1], tok(1))
         mixbuf[2 * c] = mixed[:dim]
 
+    mix_t[dim:, :] = jnp.ones((ONES, mix_t.shape[1]), jnp.bfloat16)
+
+    def decode_half(part):
+        span = n_tok // 2
+        for k in range(part * span, (part + 1) * span):
+            if k % 2:
+                arrived(("mx", k // 2), mixbuf.at[k], tok(1))
+            block = mixbuf[k]
+            mix_t[0:dim, k * rows : (k + 1) * rows] = block
+            mix[k * rows : (k + 1) * rows, :] = block.T
+        low, high = part * span * rows, (part + 1) * span * rows
+
+        def unit(i):
+            c = pairs - 1 - i
+            q = oqbuf[2 * c * qrows : (2 * c + 2) * qrows, :]
+            return mix[low:high, :], mix_t[:, low:high], q, factor
+
+        def keep(i, n, m, l):
+            dec_n[i] = n
+            dec_s[i, 0:1, :] = m
+            dec_s[i, 8:9, :] = l
+
+        def finish(i, n, m, l):
+            c = pairs - 1 - i
+            m0 = dec_s[i, 0:1, :]
+            top = jnp.maximum(m, m0)
+            a, a0 = jnp.exp2(m - top), jnp.exp2(m0 - top)
+            den = l * a + dec_s[i, 8:9, :] * a0
+            o = (n * (a / den) + dec_n[i] * (a0 / den)).T
+            for k in (2 * c, 2 * c + 1):
+                rows_k = o[(k - 2 * c) * qrows : (k - 2 * c + 1) * qrows]
+                if k == 0:
+                    out_ref[0, :, own_cols] = rows_k
+                else:
+                    osend[k] = rows_k.astype(jnp.bfloat16)
+                    send(("out", k), osend.at[k], obuf.at[k], tok(k))
+
+        units = [functools.partial(unit, i) for i in range(pairs)]
+        attend_units(units, finish if part else keep)
+
+    for k in range(1, n_tok):
+        arrived(("oq", k), oqbuf.at[pl.ds(k * qrows, qrows), :], tok(k))
+
     @pl.when(middle)
     def _():
         pass_on(3)
@@ -502,6 +546,8 @@
 
     finish_rows(0)
     mix_rows(2)
+    finish_rows(1)
+    decode_half(0)
 
     @pl.when(jnp.logical_not(middle))
     def _():
@@ -509,35 +555,10 @@
             arrived(("lz", 3, g), lat_part(3, g), tok(2))
 
     mix_rows(3)
-    for c in range(1, pairs):
+    for c in range(pairs // 2, pairs):
         finish_rows(c)
-    for k in range(n_tok):
-        if k % 2:
-            arrived(("mx", k // 2), mixbuf.at[k], tok(1))
-        block = mixbuf[k]
-        mix_t[0:dim, k * rows : (k + 1) * rows] = block
-        mix[k * rows : (k + 1) * rows, :] = block.T
-
-    for k in range(1, n_tok):
-        arrived(("oq", k), oqbuf.at[pl.ds(k * qrows, qrows), :], tok(k))
-    mix_t[dim:, :] = jnp.ones((ONES, mix_t.shape[1]), jnp.bfloat16)
-
-    def decode_unit(i):
-        c = pairs - 1 - i
-        return mix[...], mix_t[...], oqbuf[2 * c * qrows : (2 * c + 2) * qrows, :], factor
-
-    def decode_finish(i, n, m, l):
-        c = pairs - 1 - i
-        o = (n / l).T
-        for k in (2 * c, 2 * c + 1):
-            part = o[(k - 2 * c) * qrows : (k - 2 * c + 1) * qrows]
-            if k == 0:
-                out_ref[0, :, own_cols] = part
-            else:
-                osend[k] = part.astype(jnp.bfloat16)
-                send(("out", k), osend.at[k], obuf.at[k], tok(k))
-
-    attend_units([functools.partial(decode_unit, i) for i in range(pairs)], decode_finish)
+    decode_half(1)
+
     for k in range(n_tok - 1, 0, -1):
         arrived(("out", k), obuf.at[k], tok(k))
         cols = pl.ds(pl.multiple_of(peer[k] * dim, dim), dim)
@@ -601,6 +622,7 @@
         vmem((dim + ONES, n_tok * rows), bf16),
         vmem((n_tok * rows, dim), bf16),
         vmem((n_tok * qrows, dim), bf16),
+        vmem((pairs, dim, 2 * qrows), f32), vmem((pairs, 16, 2 * qrows), f32),
         vmem((n_tok, qrows, dim), bf16),
         vmem((n_tok, qrows, dim), bf16),
         pltpu.SemaphoreType.DMA((n_ids,)),

time: 91 us -> 93 us (1.022)
  Pallas kernels: 88.5 us -> 91 us
    pallas_call x1, Pallas kernels: 88.5 us -> 91 us  [local_fused(): pl.pallas_call(functools.partial(window_kernel, n_tok, n_frame), out_shap...]
where the time goes in v5:
time: 93 us; the launch traced here: 92.9 us
  Pallas kernels  91 us (98%)
  local copies, waits for them, and re-layouts  1.89 us (2%)
    pallas_call x1, Pallas kernels, local_fused(): pl.pallas_call(functools.partial(window_kernel, n_tok, n_frame), out_shap...  91 us
    unnamed x1, local copies, waits for them, and re-layouts  1.89 us

profile of v5, /device:TPU:4, one launch (start us, length us, event | category | flops | bytes accessed | tf_op | source)
XLA Modules:
  0.0 92.9 jit_solution(16556367926444889928)
XLA Ops:
  0.0 91.0 %shard_map.64 = f32[1,128,1024]{2,1,0:T(8,128)} custom-call(bf16[1,768,512]{2,1,0:T(8,128)(2,1)} %x_ref.1, bf16[512,2048]{1,0:T(8,128)(2,1)} %kvw_ref.1, bf16[128,1024]{1,0:T(8,128)(2,1)} %lq_ref.1, f32[3072]{0:T(1024)} %gain_ref.1, bf16[3072,128]{1,0:T(8,128)(2,1)} %w_ref.1, bf16[1,128,1024]{2,1,0:T(8,128)(2,1)} %oq_ref.1), custom_call_target="tpu_custom_call" | custom-call | tf_op jit(solution)/shard_map/pallas_call | solution.py:631
  91.0 1.9 %copy.8 = f32[1,128,1024]{2,1,0:T(8,128)} copy(f32[1,128,1024]{2,1,0:T(8,128)} %shard_map.64) | data formatting | bytes 1048576
